TPU v7x, 128 devices: a whole 4x4x4 slice. The times are simulated.
128 devices in a mesh: ctx: 64 (over y, z, x), tp: 2 (over core).
Axes of the slice: x: 4, y: 4, z: 4, core: 2. Of those that a mesh axis runs over, the one named last changes fastest.
Arguments:
- streams: bfloat16 [8192, 3, 8192], P('ctx', None, 'tp'), may hold values from -5 to 5
- short_taps: float32 [7, 3, 8192], P(None, None, 'tp'), may hold values from -1.6 to 1.6
- rates: float32 [16, 8192], P(None, 'tp'), may hold values from 1.2207031e-06 to 0.08
- residues: float32 [16, 8192], P(None, 'tp'), may hold values from -1 to 1
- residual: bfloat16 [8192, 8192], P('ctx', 'tp'), may hold values from -12 to 12
- gain: float32 [8192], P('tp'), may hold values from 0.5 to 1.5
- queries: bfloat16 [8192, 8192], P('ctx', 'tp'), may hold values from -100 to 100
- keys_values: bfloat16 [8192, 2, 1024], P('ctx', None, 'tp'), may hold values from -10 to 10
- lengths: int32 [4], replicated, may hold values from 1 to 4224, 8192 in all
Outputs:
- stream: bfloat16 [8192, 8192], P('ctx', 'tp')
- normed: bfloat16 [8192, 8192], P('ctx', 'tp')
- attended: bfloat16 [8192, 8192], P('ctx', 'tp')
Inputs may be any that keep to these rules, and one draw needn't show every extreme that they name: `lengths`: the longest document has exactly 4224 positions.
All inputs are finite; a program needn't handle non-finite values.
Results may differ from a plain program's by a relative error of at most 0.007.
Values may be sent and summed in bfloat16 or wider, within the bound.
No kernel may reach another device: no remote copies, remote signals or barrier semaphores. Data moves between devices by JAX's collectives and lax.ppermute only.
A program may use at most 192 MiB of HBM per device.

v0:
```python
import math

import jax
import jax.numpy as jnp
from jax import lax
from jax.sharding import PartitionSpec as P

HEAD = 128
SHORT = 7


def shifted(block, axis, distance):
    devices = range(lax.axis_size(axis))
    route = [(i - distance, i) for i in devices if i - distance in devices]
    return lax.ppermute(block, axis, route)


def entering_2(value, axis, join, neutral):
    place = lax.axis_index(axis)
    gathered = jax.tree.map(
        lambda a, kind: lax.all_gather(a.astype(kind), axis), value, (jnp.bfloat16, jnp.bfloat16)
    )
    state = jax.tree.map(lambda a, e: jnp.zeros_like(a) + jnp.asarray(e, a.dtype), value, neutral)

    def one(step, state):
        return join(
            state,
            jax.tree.map(
                lambda a, own: lax.dynamic_index_in_dim(a, step, 0, False).astype(own.dtype),
                gathered,
                value,
            ),
        )

    return lax.fori_loop(0, place, one, state)


def document_of(positions, lengths):
    bounds = jnp.cumsum(lengths)
    return jnp.sum((positions[:, None] >= bounds[None, :]).astype(jnp.int32), axis=1)


def local(streams, short_taps, rates, residues, residual, gain, queries, keys_values, lengths):
    rows_here = streams.shape[0]
    width = streams.shape[2]
    modes_here = rates.shape[0]
    ctx_index = lax.axis_index("ctx")
    kv_local = keys_values.shape[2] // HEAD
    head_local = queries.shape[1] // HEAD
    group = head_local // kv_local
    grouped = queries.reshape(rows_here, kv_local, group, HEAD)
    query_pos = ctx_index * rows_here + jnp.arange(rows_here, dtype=jnp.int32)
    query_doc = document_of(query_pos, lengths)
    last_query = ctx_index * rows_here + rows_here - 1
    factor_scale = 1.0 / math.sqrt(HEAD)

    def attend_block(state, block, block_start):

        def compute(state):
            largest, totals, accum = state
            keys = block[:, 0].reshape(-1, kv_local, HEAD)
            values = block[:, 1].reshape(-1, kv_local, HEAD)
            key_pos = block_start + jnp.arange(block.shape[0], dtype=jnp.int32)
            key_doc = document_of(key_pos, lengths)
            allowed = (key_pos[None, :] <= query_pos[:, None]) & (
                key_doc[None, :] == query_doc[:, None]
            )
            allowed = allowed[:, None, None, :]
            scores = (
                jnp.einsum("tkgd,skd->tkgs", grouped, keys, preferred_element_type=jnp.float32)
                * factor_scale
            )
            fresh = jnp.maximum(largest, jnp.max(jnp.where(allowed, scores, -1e30), axis=-1))
            weights = jnp.where(allowed, jnp.exp(scores - fresh[..., None]), 0.0)
            shrink = jnp.exp(largest - fresh)
            added = jnp.einsum(
                "tkgs,skd->tkgd",
                weights.astype(jnp.bfloat16),
                values,
                preferred_element_type=jnp.float32,
            )
            return (
                fresh,
                totals * shrink + jnp.sum(weights, axis=-1),
                accum * shrink[..., None] + added,
            )

        useful = (block_start >= 0) & (block_start <= last_query)
        return lax.cond(useful, compute, lambda kept: kept, state)

    initial = (
        jnp.full((rows_here, kv_local, group), -1e30, jnp.float32),
        jnp.zeros((rows_here, kv_local, group), jnp.float32),
        jnp.zeros((rows_here, kv_local, group, HEAD), jnp.float32),
    )
    state = initial
    rows = lax.all_gather(keys_values, "ctx", axis=0, tiled=True)
    count = rows.shape[0]
    size = math.gcd(count, 512)
    split = rows.reshape(count // size, size, 2, rows.shape[2])

    def through(state, item):
        block, number = item
        return (attend_block(state, block, number * size), None)

    state, unused = lax.scan(through, state, (split, jnp.arange(count // size, dtype=jnp.int32)))
    largest, totals, accum = state
    attended = (
        (accum / totals[..., None]).astype(jnp.bfloat16).reshape(rows_here, head_local * HEAD)
    )
    edge_rows = shifted(streams[rows_here - (SHORT - 1) :], "ctx", 1)
    window = jnp.concatenate([edge_rows, streams], axis=0).astype(jnp.float32)
    filtered = jnp.zeros((rows_here, 3, width), jnp.float32)
    for offset in range(SHORT):
        filtered = (
            filtered
            + short_taps[offset] * window[SHORT - 1 - offset : SHORT - 1 - offset + rows_here]
        )
    gated = filtered[:, 1] * filtered[:, 2]
    mode_weight = residues * jnp.sqrt(-jnp.expm1(-2.0 * rates))
    span = 16
    blocks_here = rows_here // span
    pieces = gated.reshape(blocks_here, span, width)
    local_out = jnp.zeros((blocks_here, span, width), jnp.float32)
    block_ends = jnp.zeros((blocks_here, modes_here, width), jnp.float32)
    for offset in range(span):
        tap_row = jnp.sum(mode_weight * jnp.exp(-rates * offset), axis=0)
        moved = jnp.concatenate(
            [jnp.zeros((blocks_here, offset, width), jnp.float32), pieces[:, : span - offset]],
            axis=1,
        )
        local_out = local_out + tap_row * moved
        block_ends = (
            block_ends + jnp.exp(-rates * (span - 1 - offset))[None] * pieces[:, offset][:, None, :]
        )
    stride = jnp.exp(-rates * span)

    def carry_on(entering, piece_end):
        return (stride * entering + piece_end, entering)

    device_end, entering = lax.scan(
        carry_on, jnp.zeros((modes_here, width), jnp.float32), block_ends
    )

    def combine(earlier, later):
        return (earlier[0] + later[0], jnp.exp(-rates * later[0]) * earlier[1] + later[1])

    counted = jnp.full((1,), float(rows_here), jnp.float32)
    before = entering_2(
        (counted, device_end),
        "ctx",
        combine,
        (jnp.zeros((1,), jnp.float32), jnp.zeros_like(device_end)),
    )
    incoming = before[1]
    starts = (span * jnp.arange(blocks_here)).astype(jnp.float32)
    entering = entering + jnp.exp(-rates[None] * starts[:, None, None]) * incoming[None]
    carried = jnp.stack(
        [
            jnp.sum((mode_weight * jnp.exp(-rates * (offset + 1)))[None] * entering, axis=1)
            for offset in range(span)
        ],
        axis=1,
    )
    long_out = (local_out + carried).reshape(rows_here, width)
    stream = (
        residual.astype(jnp.float32) + attended.astype(jnp.float32) + filtered[:, 0] * long_out
    ).astype(jnp.bfloat16)
    wide = stream.astype(jnp.float32)
    squares = lax.psum(jnp.sum(wide * wide, axis=1), "tp")
    mean_square = squares / (width * lax.axis_size("tp"))
    normed = (wide * lax.rsqrt(mean_square[:, None] + 1e-06) * gain).astype(jnp.bfloat16)
    return (stream, normed, attended)


def solution(mesh):
    in_specs = (
        P("ctx", None, "tp"),
        P(None, None, "tp"),
        P(None, "tp"),
        P(None, "tp"),
        P("ctx", "tp"),
        P("tp"),
        P("ctx", "tp"),
        P("ctx", None, "tp"),
        P(),
    )
    out_specs = (P("ctx", "tp"), P("ctx", "tp"), P("ctx", "tp"))
    return jax.shard_map(local, mesh=mesh, in_specs=in_specs, out_specs=out_specs, check_vma=False)
```

profile of v0, /device:TPU:127, one launch (start us, length us, event | category | flops | bytes accessed | tf_op | source)
XLA Modules:
  0.0 732.6 jit_solution(1813009395057907764)
XLA Ops:
  9.5 2.7 fusion.76
  12.2 1.9 multiply_reduce_fusion.16
  14.3 4.0 fusion.45
  18.4 2.9 maximum_convert_fusion
  21.3 5.2 fusion.17
  26.7 2.4 copy-done
  29.0 2.1 fusion.75
  33.2 3.4 multiply_add_fusion.2
  36.7 14.9 %while.44 = (s32[]{:T(128)}, f32[16,4096]{1,0:T(8,128)S(1)}, f32[8,16,4096]{2,1,0:T(8,128)}, f32[16,4096]{1,0:T(8,128)S(1)}, f32[8,16,4096]{2,1,0:T(8,128)}, /*index=5*/s32[]{:T(128)}, s32[]{:T(128)}) while((s32[]{:T(128)}, f32[16,4096]{1,0:T(8,128)S(1)}, f32[8,16,4096]{2,1,0:T(8,128)}, f32[16,4096]{1,0:T(8,128)S(1)}, ...), condition=%wide.region_27.28_spmd.clone, body=%wide.region_26.27_spmd.clone.sunk | while | flops 262147 | bytes 1572968 | solution.py:141
  53.8 2.3 copy.32
  59.4 1.9 dynamic-update-slice
  61.3 146.2 %all-reduce.15 = bf16[64]{0:T(256)(128)(2,1)} all-reduce(bf16[64]{0:T(256)(128)(2,1)} %dynamic-update-slice), channel_id=1, replica_groups=mesh['ctx'=64,'tp'=2] {'ctx'}, use_global_device_ids=true, to_apply=%add.15 | all-reduce | flops 64 | bytes 256
  216.7 223.7 %while.42 = (s32[]{:T(128)}, f32[16,4096]{1,0:T(8,128)}, s32[]{:T(128)}, bf16[64,1]{0,1:T(2,128)(2,1)}, f32[16,4096]{1,0:T(8,128)S(1)}, /*index=5*/bf16[64,16,4096]{2,1,0:T(8,128)(2,1)}, s32[]{:T(128)}, s32[]{:T(128)}, s32[]{:T(128)}) while((s32[]{:T(128)}, f32[16,4096]{1,0:T(8,128)}, s32[]{:T(128)}, bf16[64,1]{0,1:T(2,128)(2,1)}, ...), condition=%wide.region_29.30_spmd, body=%wide.region_28.29_spmd.sunk | while | flops 262150 | bytes 917661 | solution.py:35
  440.4 10.4 %multiply_reduce_fusion = (f32[8,4096]{1,0:T(8,128)S(1)}, f32[8,4096]{1,0:T(8,128)S(1)}, f32[8,4096]{1,0:T(8,128)S(1)}, f32[8,4096]{1,0:T(8,128)S(1)}, f32[8,409...) fusion(f32[16,4096]{1,0:T(8,128)} %get-tuple-element.476, ...), kind=kLoop, calls=%fused_computation.51 | loop fusion | flops 17825792 | bytes 8912928 | tf_op jit(solution)/shard_map/reduce_sum | solution.py:160
  462.7 7.8 %stack.67 = f32[8,16,4096]{2,1,0:T(8,128)} concatenate(f32[8,1,4096]{2,1,0:T(1,128)} %stack.51, f32[8,1,4096]{2,1,0:T(1,128)} %stack.52, f32[8,1,4096]{2,1,0:T(1,128)} %stack.53, f32[8,1,4096]{2,1,0:T(1,128)} %stack.54, f32[8,1,4096]{2,1,0:T(1,128)} %stack.55, f32[8,1,4096]{2,1,0:T(1,128)} %stack.56, f32[8,1,4096]{2,1,0:T(1,128)} %stack.57, f32[8,1,4096]{2,1,0:T(1,128)} %stack.58, ...), dimensions={1} | concatenate | bytes 4194304 | tf_op jit(solution)/shard_map/stack | solution.py:158
  470.6 7.5 %add_add_fusion = f32[8,16,4096]{2,1,0:T(8,128)} fusion(f32[8,16,4096]{2,1,0:T(8,128)} %stack.67, f32[8,1,4096]{2,1,0:T(1,128)S(1)} %get-tuple-element.432, f32[8,2,4096]{2,1,0:T(2,128)S(1)} %copy-done.3, f32[8,3,4096]{2,1,0:T(4,128)} %slice.225, f32[8,4,4096]{2,1,0:T(4,128)} %slice.224, f32[8,5,4096]{2,1,0:T(8,128)} %slice.223, f32[8,6,4096]{2,1,0:T(8,128)} %slice.222, ...), kind=kLoop, calls=%fused_computation.69 | loop fusion | flops 16777216 | bytes 22282240 | tf_op jit(solution)/shard_map/add | solution.py:165
  478.1 23.7 %copy.33 = bf16[16,512,2,512]{1,3,2,0:T(8,128)(2,1)} copy(bf16[16,512,2,512]{3,1,0,2:T(8,128)(2,1)} %bitcast.167) | data formatting | bytes 33554432
  503.4 184.1 %while.43 = (s32[]{:T(128)}, f32[128,4,8]{0,2,1:T(8,128)S(1)}, f32[128,4,8]{0,2,1:T(8,128)S(1)}, f32[128,4,8,128]{3,0,2,1:T(8,128)}, s32[16]{0:T(128)S(1)}, /*in...) while((s32[]{:T(128)}, f32[128,4,8]{0,2,1:T(8,128)S(1)}, ...), condition=%wide.region_9.10_spmd.clone, body=%wide.region_2.9_spmd.clone.sunk | while | flops 1098070144 | bytes 36189072 | solution.py:106
  504.7 10.3 %conditional.3 = ((f32[128,4,8]{0,2,1:T(8,128)S(1)}, f32[128,4,8]{0,2,1:T(8,128)S(1)}, f32[128,4,8,128]{3,0,2,1:T(8,128)})) conditional(s32[]{:T(128)} %convert_element_type.96, (f32[128,4,8]{0,2,1:T(8,128)S(1)}, f32[128,4,8]{0,2,1:T(8,128)S(1)}, f32[128,4,8,128]{3,0,2,1:T(8,128)}) %tuple.187, (s32[]{:T(128)}, s32[]{:T(128)}, s32[4]{0:T(128)S(1)}, ...), branch_computations={%region_3.3_spmd, %region_4.8_spmd} | conditional | flops 1098070144 | bytes 36188256 | solution.py:89
  508.0 1.8 fusion.6
  509.9 5.0 bitcast_add_fusion
  516.2 10.3 %conditional.3 = ((f32[128,4,8]{0,2,1:T(8,128)S(1)}, f32[128,4,8]{0,2,1:T(8,128)S(1)}, f32[128,4,8,128]{3,0,2,1:T(8,128)})) conditional(s32[]{:T(128)} %convert_element_type.96, (f32[128,4,8]{0,2,1:T(8,128)S(1)}, f32[128,4,8]{0,2,1:T(8,128)S(1)}, f32[128,4,8,128]{3,0,2,1:T(8,128)}) %tuple.187, (s32[]{:T(128)}, s32[]{:T(128)}, s32[4]{0:T(128)S(1)}, ...), branch_computations={%region_3.3_spmd, %region_4.8_spmd} | conditional | flops 1098070144 | bytes 36188256 | solution.py:89
  519.5 1.8 fusion.6
  521.4 5.0 bitcast_add_fusion
  527.7 10.3 %conditional.3 = ((f32[128,4,8]{0,2,1:T(8,128)S(1)}, f32[128,4,8]{0,2,1:T(8,128)S(1)}, f32[128,4,8,128]{3,0,2,1:T(8,128)})) conditional(s32[]{:T(128)} %convert_element_type.96, (f32[128,4,8]{0,2,1:T(8,128)S(1)}, f32[128,4,8]{0,2,1:T(8,128)S(1)}, f32[128,4,8,128]{3,0,2,1:T(8,128)}) %tuple.187, (s32[]{:T(128)}, s32[]{:T(128)}, s32[4]{0:T(128)S(1)}, ...), branch_computations={%region_3.3_spmd, %region_4.8_spmd} | conditional | flops 1098070144 | bytes 36188256 | solution.py:89
  531.1 1.8 fusion.6
  532.9 5.0 bitcast_add_fusion
  539.2 10.3 %conditional.3 = ((f32[128,4,8]{0,2,1:T(8,128)S(1)}, f32[128,4,8]{0,2,1:T(8,128)S(1)}, f32[128,4,8,128]{3,0,2,1:T(8,128)})) conditional(s32[]{:T(128)} %convert_element_type.96, (f32[128,4,8]{0,2,1:T(8,128)S(1)}, f32[128,4,8]{0,2,1:T(8,128)S(1)}, f32[128,4,8,128]{3,0,2,1:T(8,128)}) %tuple.187, (s32[]{:T(128)}, s32[]{:T(128)}, s32[4]{0:T(128)S(1)}, ...), branch_computations={%region_3.3_spmd, %region_4.8_spmd} | conditional | flops 1098070144 | bytes 36188256 | solution.py:89
  542.6 1.8 fusion.6
  544.4 5.0 bitcast_add_fusion
  550.7 10.3 %conditional.3 = ((f32[128,4,8]{0,2,1:T(8,128)S(1)}, f32[128,4,8]{0,2,1:T(8,128)S(1)}, f32[128,4,8,128]{3,0,2,1:T(8,128)})) conditional(s32[]{:T(128)} %convert_element_type.96, (f32[128,4,8]{0,2,1:T(8,128)S(1)}, f32[128,4,8]{0,2,1:T(8,128)S(1)}, f32[128,4,8,128]{3,0,2,1:T(8,128)}) %tuple.187, (s32[]{:T(128)}, s32[]{:T(128)}, s32[4]{0:T(128)S(1)}, ...), branch_computations={%region_3.3_spmd, %region_4.8_spmd} | conditional | flops 1098070144 | bytes 36188256 | solution.py:89
  554.1 1.8 fusion.6
  555.9 5.0 bitcast_add_fusion
  562.2 10.3 %conditional.3 = ((f32[128,4,8]{0,2,1:T(8,128)S(1)}, f32[128,4,8]{0,2,1:T(8,128)S(1)}, f32[128,4,8,128]{3,0,2,1:T(8,128)})) conditional(s32[]{:T(128)} %convert_element_type.96, (f32[128,4,8]{0,2,1:T(8,128)S(1)}, f32[128,4,8]{0,2,1:T(8,128)S(1)}, f32[128,4,8,128]{3,0,2,1:T(8,128)}) %tuple.187, (s32[]{:T(128)}, s32[]{:T(128)}, s32[4]{0:T(128)S(1)}, ...), branch_computations={%region_3.3_spmd, %region_4.8_spmd} | conditional | flops 1098070144 | bytes 36188256 | solution.py:89
  565.6 1.8 fusion.6
  567.4 5.0 bitcast_add_fusion
  573.7 10.3 %conditional.3 = ((f32[128,4,8]{0,2,1:T(8,128)S(1)}, f32[128,4,8]{0,2,1:T(8,128)S(1)}, f32[128,4,8,128]{3,0,2,1:T(8,128)})) conditional(s32[]{:T(128)} %convert_element_type.96, (f32[128,4,8]{0,2,1:T(8,128)S(1)}, f32[128,4,8]{0,2,1:T(8,128)S(1)}, f32[128,4,8,128]{3,0,2,1:T(8,128)}) %tuple.187, (s32[]{:T(128)}, s32[]{:T(128)}, s32[4]{0:T(128)S(1)}, ...), branch_computations={%region_3.3_spmd, %region_4.8_spmd} | conditional | flops 1098070144 | bytes 36188256 | solution.py:89
  577.1 1.8 fusion.6
  578.9 5.0 bitcast_add_fusion
  585.2 10.3 %conditional.3 = ((f32[128,4,8]{0,2,1:T(8,128)S(1)}, f32[128,4,8]{0,2,1:T(8,128)S(1)}, f32[128,4,8,128]{3,0,2,1:T(8,128)})) conditional(s32[]{:T(128)} %convert_element_type.96, (f32[128,4,8]{0,2,1:T(8,128)S(1)}, f32[128,4,8]{0,2,1:T(8,128)S(1)}, f32[128,4,8,128]{3,0,2,1:T(8,128)}) %tuple.187, (s32[]{:T(128)}, s32[]{:T(128)}, s32[4]{0:T(128)S(1)}, ...), branch_computations={%region_3.3_spmd, %region_4.8_spmd} | conditional | flops 1098070144 | bytes 36188256 | solution.py:89
  588.6 1.8 fusion.6
  590.4 5.0 bitcast_add_fusion
  596.7 10.3 %conditional.3 = ((f32[128,4,8]{0,2,1:T(8,128)S(1)}, f32[128,4,8]{0,2,1:T(8,128)S(1)}, f32[128,4,8,128]{3,0,2,1:T(8,128)})) conditional(s32[]{:T(128)} %convert_element_type.96, (f32[128,4,8]{0,2,1:T(8,128)S(1)}, f32[128,4,8]{0,2,1:T(8,128)S(1)}, f32[128,4,8,128]{3,0,2,1:T(8,128)}) %tuple.187, (s32[]{:T(128)}, s32[]{:T(128)}, s32[4]{0:T(128)S(1)}, ...), branch_computations={%region_3.3_spmd, %region_4.8_spmd} | conditional | flops 1098070144 | bytes 36188256 | solution.py:89
  600.1 1.8 fusion.6
  601.9 5.0 bitcast_add_fusion
  608.2 10.3 %conditional.3 = ((f32[128,4,8]{0,2,1:T(8,128)S(1)}, f32[128,4,8]{0,2,1:T(8,128)S(1)}, f32[128,4,8,128]{3,0,2,1:T(8,128)})) conditional(s32[]{:T(128)} %convert_element_type.96, (f32[128,4,8]{0,2,1:T(8,128)S(1)}, f32[128,4,8]{0,2,1:T(8,128)S(1)}, f32[128,4,8,128]{3,0,2,1:T(8,128)}) %tuple.187, (s32[]{:T(128)}, s32[]{:T(128)}, s32[4]{0:T(128)S(1)}, ...), branch_computations={%region_3.3_spmd, %region_4.8_spmd} | conditional | flops 1098070144 | bytes 36188256 | solution.py:89
  613.5 5.0 bitcast_add_fusion
  619.7 10.3 %conditional.3 = ((f32[128,4,8]{0,2,1:T(8,128)S(1)}, f32[128,4,8]{0,2,1:T(8,128)S(1)}, f32[128,4,8,128]{3,0,2,1:T(8,128)})) conditional(s32[]{:T(128)} %convert_element_type.96, (f32[128,4,8]{0,2,1:T(8,128)S(1)}, f32[128,4,8]{0,2,1:T(8,128)S(1)}, f32[128,4,8,128]{3,0,2,1:T(8,128)}) %tuple.187, (s32[]{:T(128)}, s32[]{:T(128)}, s32[4]{0:T(128)S(1)}, ...), branch_computations={%region_3.3_spmd, %region_4.8_spmd} | conditional | flops 1098070144 | bytes 36188256 | solution.py:89
  625.0 5.0 bitcast_add_fusion
  631.3 10.3 %conditional.3 = ((f32[128,4,8]{0,2,1:T(8,128)S(1)}, f32[128,4,8]{0,2,1:T(8,128)S(1)}, f32[128,4,8,128]{3,0,2,1:T(8,128)})) conditional(s32[]{:T(128)} %convert_element_type.96, (f32[128,4,8]{0,2,1:T(8,128)S(1)}, f32[128,4,8]{0,2,1:T(8,128)S(1)}, f32[128,4,8,128]{3,0,2,1:T(8,128)}) %tuple.187, (s32[]{:T(128)}, s32[]{:T(128)}, s32[4]{0:T(128)S(1)}, ...), branch_computations={%region_3.3_spmd, %region_4.8_spmd} | conditional | flops 1098070144 | bytes 36188256 | solution.py:89
  634.6 1.8 fusion.6
  636.5 5.0 bitcast_add_fusion
  642.8 10.3 %conditional.3 = ((f32[128,4,8]{0,2,1:T(8,128)S(1)}, f32[128,4,8]{0,2,1:T(8,128)S(1)}, f32[128,4,8,128]{3,0,2,1:T(8,128)})) conditional(s32[]{:T(128)} %convert_element_type.96, (f32[128,4,8]{0,2,1:T(8,128)S(1)}, f32[128,4,8]{0,2,1:T(8,128)S(1)}, f32[128,4,8,128]{3,0,2,1:T(8,128)}) %tuple.187, (s32[]{:T(128)}, s32[]{:T(128)}, s32[4]{0:T(128)S(1)}, ...), branch_computations={%region_3.3_spmd, %region_4.8_spmd} | conditional | flops 1098070144 | bytes 36188256 | solution.py:89
  648.0 5.0 bitcast_add_fusion
  654.3 10.3 %conditional.3 = ((f32[128,4,8]{0,2,1:T(8,128)S(1)}, f32[128,4,8]{0,2,1:T(8,128)S(1)}, f32[128,4,8,128]{3,0,2,1:T(8,128)})) conditional(s32[]{:T(128)} %convert_element_type.96, (f32[128,4,8]{0,2,1:T(8,128)S(1)}, f32[128,4,8]{0,2,1:T(8,128)S(1)}, f32[128,4,8,128]{3,0,2,1:T(8,128)}) %tuple.187, (s32[]{:T(128)}, s32[]{:T(128)}, s32[4]{0:T(128)S(1)}, ...), branch_computations={%region_3.3_spmd, %region_4.8_spmd} | conditional | flops 1098070144 | bytes 36188256 | solution.py:89
  659.5 5.0 bitcast_add_fusion
  665.8 10.3 %conditional.3 = ((f32[128,4,8]{0,2,1:T(8,128)S(1)}, f32[128,4,8]{0,2,1:T(8,128)S(1)}, f32[128,4,8,128]{3,0,2,1:T(8,128)})) conditional(s32[]{:T(128)} %convert_element_type.96, (f32[128,4,8]{0,2,1:T(8,128)S(1)}, f32[128,4,8]{0,2,1:T(8,128)S(1)}, f32[128,4,8,128]{3,0,2,1:T(8,128)}) %tuple.187, (s32[]{:T(128)}, s32[]{:T(128)}, s32[4]{0:T(128)S(1)}, ...), branch_computations={%region_3.3_spmd, %region_4.8_spmd} | conditional | flops 1098070144 | bytes 36188256 | solution.py:89
  669.1 1.8 fusion.6
  671.0 5.0 bitcast_add_fusion
  677.3 10.3 %conditional.3 = ((f32[128,4,8]{0,2,1:T(8,128)S(1)}, f32[128,4,8]{0,2,1:T(8,128)S(1)}, f32[128,4,8,128]{3,0,2,1:T(8,128)})) conditional(s32[]{:T(128)} %convert_element_type.96, (f32[128,4,8]{0,2,1:T(8,128)S(1)}, f32[128,4,8]{0,2,1:T(8,128)S(1)}, f32[128,4,8,128]{3,0,2,1:T(8,128)}) %tuple.187, (s32[]{:T(128)}, s32[]{:T(128)}, s32[4]{0:T(128)S(1)}, ...), branch_computations={%region_3.3_spmd, %region_4.8_spmd} | conditional | flops 1098070144 | bytes 36188256 | solution.py:89
  682.5 5.0 bitcast_add_fusion
  687.5 2.1 divide_convert_fusion
  690.4 3.6 fusion.23
  694.0 30.4 %psum.7 = f32[128]{0:T(128)S(1)} all-reduce(f32[128]{0:T(128)S(1)} %get-tuple-element.393), channel_id=1, replica_groups=mesh['ctx'=64,'tp'=2] {'tp'}, use_global_device_ids=true, to_apply=%region_47.48 | all-reduce | flops 128 | bytes 1024 | tf_op jit(solution)/shard_map/psum | solution.py:170
  (478 shorter events, 309.0 us)
Async XLA Ops:
  7.2 7.1 copy-start.5
  7.2 208.8 %all-gather.6.cloned.1.call-start = ((), (), s32[]{:S(2)}) async-start(), calls=%async_computation.1 | async-start | bytes 8519680 | tf_op jit(solution)/shard_map/all_gather | solution.py:21
  8.2 10.1 %collective-permute-start = (bf16[6,3,4096]{2,0,1:T(8,128)(2,1)S(1)}, bf16[6,3,4096]{2,0,1:T(8,128)(2,1)S(1)}, u32[]{:S(2)}, u32[]{:S(2)}) collective-permute-start(bf16[6,3,4096]{2,0,1:T(8,128)(2,1)S(1)} %slice.154), channel_id=1, source_target_pairs={{0,2},{2,4},{4,6},{6,8},{8,10},{10,12},{12,14},{14,16},{16,18},{18... | collective-permute-start | bytes 442376 | tf_op jit(solution)/shard_map/ppermute | solution.py:15
  26.4 2.6 copy-start
  31.1 1.6 copy-start.6
  31.2 1.6 copy-start.7
  31.2 1.6 copy-start.8
  31.2 1.6 copy-start.9
  31.2 1.6 copy-start.10
  31.2 1.6 copy-start.11
  31.2 1.6 copy-start.12
  31.2 1.6 copy-start.13
  31.2 1.6 copy-start.14
  31.2 1.6 copy-start.15
  31.2 1.7 copy-start.16
  31.3 1.7 copy-start.17
  31.3 1.8 copy-start.18
  31.3 1.9 copy-start.19
  31.3 1.9 copy-start.20
  36.7 15.6 %copy-start.21 = (bf16[128,2,512]{2,1,0:T(2,128)(2,1)S(1)}, bf16[128,2,512]{2,1,0:T(2,128)(2,1)}, u32[]{:S(2)}) copy-start(bf16[128,2,512]{2,1,0:T(2,128)(2,1)} %param.24) | copy-start | bytes 786436
  36.7 16.4 %copy-start.24 = (s32[4]{0:T(128)S(1)}, s32[4]{0:T(128)}, u32[]{:S(2)}) copy-start(s32[4]{0:T(128)} %param.25) | copy-start | bytes 52
  52.2 425.9 %all-gather.4.cloned.1.call-start = ((), (), s32[]{:S(2)}) async-start(), calls=%async_computation | async-start | bytes 17039360 | tf_op jit(solution)/shard_map/all_gather | solution.py:97
  462.7 7.8 %copy-start.3 = (f32[8,2,4096]{2,1,0:T(2,128)S(1)}, f32[8,2,4096]{2,1,0:T(2,128)}, u32[]{:S(2)}) copy-start(f32[8,2,4096]{2,1,0:T(2,128)} %slice.226) | copy-start | bytes 786436
  501.8 1.6 copy-start.23
  501.8 1.6 copy-start.25
  687.5 2.8 copy-start.1
  687.5 2.8 copy-start.4
  690.4 34.1 %copy-start.22 = (f32[4096]{0:T(1024)S(1)}, f32[4096]{0:T(1024)}, u32[]{:S(2)}) copy-start(f32[4096]{0:T(1024)} %param.22) | copy-start | bytes 49156
  694.0 31.7 %copy-start.2 = (bf16[128,4096]{1,0:T(8,128)(2,1)}, bf16[128,4096]{1,0:T(8,128)(2,1)S(1)}, u32[]{:S(2)}) copy-start(bf16[128,4096]{1,0:T(8,128)(2,1)S(1)} %get-tuple-element.394) | copy-start | bytes 3145732
Sparse Core Ops, SparseCore 0:
  52.4 79.8 all-gather.5
  135.1 104.3 all-gather.3
where the time goes:
time: 738 us; the launch traced here: 733 us
  other arithmetic  210 us (28%)
  local copies, waits for them, and re-layouts  179 us (24%)
  blocking collectives  177 us (24%)
  matrix products  104 us (14%)
  loops' own time  47.9 us (6%)
  between operations  14.6 us (2%)
    unnamed x1, blocking collectives  146 us
    add x63, other arithmetic, combine(): jnp.exp(-rates * later[0]) * earlier[1] + later[1]  112 us
    dot_general x16, matrix products, compute(): jnp.einsum('tkgs,skd->tkgd', weights.astype(jnp.bfloat16), values, prefer...  80.6 us
    dynamic_slice x63, local copies, waits for them, and re-layouts, one(): lax.dynamic_index_in_dim(a, step, 0, False).astype(own.dtype)  75.9 us
    unnamed x79, local copies, waits for them, and re-layouts  36.4 us
    another operation x1, loops' own time, entering_2(): return lax.fori_loop(0, place, one, state)  35.8 us
    psum x1, blocking collectives, local(): squares = lax.psum(jnp.sum(wide * wide, axis=1), 'tp')  30.4 us
    reduce_sum x16, other arithmetic, compute(): jnp.sum(weights, axis=-1)  29.3 us
  transfers between devices with their start and end apart: 3, of which 0 were waited for; matrix products, arithmetic and copies ran while one was open for 34% of the time, Pallas kernels for 0%

commit v1 on v0

v1 whole, which is shorter than its diff:
```python
import math

import jax
import jax.numpy as jnp
from jax import lax
from jax.experimental import pallas as pl
from jax.experimental.pallas import tpu as pltpu
from jax.sharding import Mesh
from jax.sharding import PartitionSpec as P

HEAD = 128
SHORT = 7
MODES = 16
ROWS = 128
SIDE = 4
LANES = 128
SUB = 8
GROUP = SUB * LANES
CHUNK = SIDE * ROWS
SCALE = math.log2(math.e) / math.sqrt(HEAD)
NEG = -1e30


def turn(value, axis, distance):
    if distance % SIDE == 0:
        return value
    return lax.ppermute(value, axis, [(i, (i + distance) % SIDE) for i in range(SIDE)])


def mixer_kernel(x_ref, halo_ref, taps_ref, decay_ref, weight_ref, residual_ref,
                 base_ref, first_ref, end_ref, window, gated, out):
    def filtered(j):
        window[0:SUB] = halo_ref[j]
        window[SUB:] = x_ref[j].astype(jnp.float32)
        total = taps_ref[j, 0:1] * window[SUB:SUB + ROWS]
        for i in range(1, SHORT):
            total = total + taps_ref[j, i:i + 1] * window[SUB - i:SUB - i + ROWS]
        return total

    first_ref[...] = filtered(1)
    product = first_ref[...] * filtered(2)
    for c in range(SUB):
        gated[pl.ds(c, ROWS, stride=SUB), :] = product[:, c * LANES:(c + 1) * LANES]
    first_ref[...] = filtered(0)

    def step(t, states):
        rows = pl.ds(pl.multiple_of(t * SUB, SUB), SUB)
        g = gated[rows, :]
        fresh = tuple(decay_ref[n] * states[n] + g for n in range(MODES))
        parts = [weight_ref[n] * fresh[n] for n in range(MODES)]
        while len(parts) > 1:
            parts = [a + b for a, b in zip(parts[::2], parts[1::2])]
        out[rows, :] = parts[0]
        return fresh

    zero = jnp.zeros((SUB, LANES), jnp.float32)
    states = lax.fori_loop(0, ROWS, step, (zero,) * MODES)
    for n in range(MODES):
        end_ref[n] = states[n]
    for c in range(SUB):
        cols = slice(c * LANES, (c + 1) * LANES)
        base_ref[:, cols] = (
            residual_ref[:, cols].astype(jnp.float32)
            + first_ref[:, cols] * out[pl.ds(c, ROWS, stride=SUB), :]
        )


def carried_kernel(state_ref, decay_ref, weight_ref, base_ref, first_ref, full_ref, out):
    def step(t, states):
        rows = pl.ds(pl.multiple_of(t * SUB, SUB), SUB)
        fresh = tuple(decay_ref[n] * states[n] for n in range(MODES))
        parts = list(fresh)
        while len(parts) > 1:
            parts = [a + b for a, b in zip(parts[::2], parts[1::2])]
        out[rows, :] = parts[0]
        return fresh

    lax.fori_loop(0, ROWS, step, tuple(weight_ref[n] * state_ref[n] for n in range(MODES)))
    for c in range(SUB):
        cols = slice(c * LANES, (c + 1) * LANES)
        full_ref[:, cols] = base_ref[:, cols] + first_ref[:, cols] * out[pl.ds(c, ROWS, stride=SUB), :]


def attend_kernel(place_ref, lengths_ref, q_ref, a0, a1, a2, a3, b0, b1, b2, b3, o_ref,
                  q_rows, keys, values, accum, largest, sems):
    y, z, x, back = place_ref[0], place_ref[1], place_ref[2], place_ref[3]
    query_block = 16 * lax.rem(y - back + SIDE, SIDE) + 4 * z + x
    query_first = query_block * ROWS
    bounds = []
    total = 0
    for i in range(4):
        total = total + lengths_ref[i]
        bounds.append(total)

    def document_start(position):
        start = jnp.zeros_like(position)
        for bound in bounds:
            start = jnp.maximum(start, jnp.where(position >= bound, bound, 0))
        return start

    first_start = document_start(query_first)
    last_start = document_start(query_first + ROWS - 1)
    top = query_block // SIDE
    low = first_start // CHUNK
    halves = ((a0, a1, a2, a3), (b0, b1, b2, b3))

    def copies(chunk, slot, act):
        plane, row = chunk // SIDE, lax.rem(chunk, SIDE)
        turned = lax.rem(y - plane + SIDE, SIDE)
        behind = lax.rem(z - row + SIDE, SIDE)

        def pair(source, k):
            target = lax.rem(x - k + SIDE, SIDE)
            rows = pl.ds(pl.multiple_of(target * ROWS, ROWS), ROWS)
            act(pltpu.make_async_copy(source.at[0], keys.at[slot, rows], sems.at[slot, k]))
            act(pltpu.make_async_copy(source.at[1], values.at[slot, rows, pl.ds(0, HEAD)], sems.at[slot, 4 + k]))

        for m in range(SIDE):
            @pl.when((turned < 2) & (behind == m))
            def _():
                for k in range(SIDE):
                    pair(halves[0][m].at[k, turned], k)

        @pl.when(turned >= 2)
        def _():
            for m in range(SIDE):
                pair(halves[1][m].at[behind, turned - 2], m)

    copies(top, 0, lambda c: c.start())
    for g in range(SUB):
        q_rows[g * ROWS:(g + 1) * ROWS] = q_ref[:, g * HEAD:(g + 1) * HEAD]
    values[:, :, HEAD:] = jnp.ones((2, CHUNK, HEAD), jnp.bfloat16)
    accum[...] = jnp.zeros_like(accum)
    largest[...] = jnp.full_like(largest, NEG)

    def one(step, carry):
        chunk = top - step
        slot = lax.rem(step, 2)

        @pl.when(chunk > low)
        def _():
            copies(chunk - 1, 1 - slot, lambda c: c.start())

        copies(chunk, slot, lambda c: c.wait())
        key_first = chunk * CHUNK
        whole = (key_first + CHUNK - 1 <= query_first) & (key_first >= last_start)

        def update(masked):
            scores = lax.dot_general(
                q_rows[...], keys[slot], (((1,), (1,)), ((), ())), preferred_element_type=jnp.float32
            )
            if masked:
                query_pos = query_first + lax.broadcasted_iota(jnp.int32, (ROWS, CHUNK), 0)
                key_pos = key_first + lax.broadcasted_iota(jnp.int32, (ROWS, CHUNK), 1)
                allowed = (key_pos <= query_pos) & (key_pos >= document_start(query_pos))
                bias = jnp.where(allowed, 0.0, NEG)
                scores = (scores.reshape(SUB, ROWS, CHUNK) + bias[None]).reshape(SUB * ROWS, CHUNK)
            before = largest[...]
            fresh = jnp.maximum(before, SCALE * jnp.max(scores, axis=1, keepdims=True))
            weights = jnp.exp2(scores * SCALE - fresh[:, 0:1]).astype(jnp.bfloat16)
            added = jnp.dot(weights, values[slot], preferred_element_type=jnp.float32)
            shrink = jnp.exp2(before - fresh)
            largest[...] = fresh
            accum[:, :HEAD] = accum[:, :HEAD] * shrink + added[:, :HEAD]
            accum[:, HEAD:] = accum[:, HEAD:] * shrink + added[:, HEAD:]

        pl.when(whole)(lambda: update(False))
        pl.when(jnp.logical_not(whole))(lambda: update(True))
        return carry

    lax.fori_loop(0, top - low + 1, one, 0)
    for g in range(SUB):
        rows = slice(g * ROWS, (g + 1) * ROWS)
        o_ref[:, g * HEAD:(g + 1) * HEAD] = (accum[rows, :HEAD] / accum[rows, HEAD:]).astype(jnp.bfloat16)


def mixer(x, halo, taps, decay, weight, residual):
    width = residual.shape[1]
    steps = width // GROUP
    flat = jax.ShapeDtypeStruct((ROWS, width), jnp.float32)
    return pl.pallas_call(
        mixer_kernel,
        grid=(steps,),
        in_specs=[
            pl.BlockSpec((3, ROWS, GROUP), lambda i: (0, 0, i)),
            pl.BlockSpec((3, SUB, GROUP), lambda i: (0, 0, i)),
            pl.BlockSpec((3, SHORT, GROUP), lambda i: (0, 0, i)),
            pl.BlockSpec((MODES, SUB, LANES), lambda i: (0, i, 0)),
            pl.BlockSpec((MODES, SUB, LANES), lambda i: (0, i, 0)),
            pl.BlockSpec((ROWS, GROUP), lambda i: (0, i)),
        ],
        out_specs=[
            pl.BlockSpec((ROWS, GROUP), lambda i: (0, i)),
            pl.BlockSpec((ROWS, GROUP), lambda i: (0, i)),
            pl.BlockSpec((MODES, SUB, LANES), lambda i: (0, i, 0)),
        ],
        out_shape=[flat, flat, jax.ShapeDtypeStruct(decay.shape, jnp.float32)],
        scratch_shapes=[
            pltpu.VMEM((SUB + ROWS, GROUP), jnp.float32),
            pltpu.VMEM((ROWS * SUB, LANES), jnp.float32),
            pltpu.VMEM((ROWS * SUB, LANES), jnp.float32),
        ],
        compiler_params=pltpu.CompilerParams(vmem_limit_bytes=32 * 1024 * 1024),
        cost_estimate=pl.CostEstimate(flops=80_000_000, bytes_accessed=10_000_000, transcendentals=0),
        name="mixer",
    )(x, halo, taps, decay, weight, residual)


def carried(state, decay, weight, base, first):
    width = base.shape[1]
    steps = width // GROUP
    modes = pl.BlockSpec((MODES, SUB, LANES), lambda i: (0, i, 0))
    rows = pl.BlockSpec((ROWS, GROUP), lambda i: (0, i))
    return pl.pallas_call(
        carried_kernel,
        grid=(steps,),
        in_specs=[modes, modes, modes, rows, rows],
        out_specs=rows,
        out_shape=jax.ShapeDtypeStruct((ROWS, width), jnp.float32),
        scratch_shapes=[pltpu.VMEM((ROWS * SUB, LANES), jnp.float32)],
        compiler_params=pltpu.CompilerParams(vmem_limit_bytes=32 * 1024 * 1024),
        cost_estimate=pl.CostEstimate(flops=20_000_000, bytes_accessed=6_000_000, transcendentals=0),
        name="carried",
    )(state, decay, weight, base, first)


def attend(place, lengths, q, blocks):
    smem = pl.BlockSpec(memory_space=pltpu.SMEM)
    vmem = pl.BlockSpec(memory_space=pltpu.VMEM)
    return pl.pallas_call(
        attend_kernel,
        in_specs=[smem, smem, vmem] + [pl.BlockSpec(memory_space=pl.ANY)] * 8,
        out_specs=vmem,
        out_shape=jax.ShapeDtypeStruct(q.shape, jnp.bfloat16),
        scratch_shapes=[
            pltpu.VMEM((SUB * ROWS, HEAD), jnp.bfloat16),
            pltpu.VMEM((2, CHUNK, HEAD), jnp.bfloat16),
            pltpu.VMEM((2, CHUNK, 2 * HEAD), jnp.bfloat16),
            pltpu.VMEM((SUB * ROWS, 2 * HEAD), jnp.float32),
            pltpu.VMEM((SUB * ROWS, LANES), jnp.float32),
            pltpu.SemaphoreType.DMA((2, 8)),
        ],
        compiler_params=pltpu.CompilerParams(vmem_limit_bytes=40 * 1024 * 1024),
        cost_estimate=pl.CostEstimate(flops=3_000_000_000, bytes_accessed=2_000_000, transcendentals=3_000_000),
        name="attend",
    )(place, lengths, q, *blocks)


def local(streams, short_taps, rates, residues, residual, gain, queries, keys_values, lengths):
    width = residual.shape[1]
    head_cols = width // SIDE
    y, z, x = (lax.axis_index(a) for a in ("y", "z", "x"))
    ctx = ("y", "z", "x")

    by_head = keys_values.reshape(ROWS, 2, SIDE, HEAD).transpose(2, 1, 0, 3)
    near = [
        turn(lax.dynamic_index_in_dim(by_head, lax.rem(y + r, SIDE), 0, False), "y", r) for r in range(SIDE)
    ]
    part_a, part_b = jnp.stack(near[:2]), jnp.stack(near[2:])
    row_a = jnp.stack([turn(part_a, "x", k) for k in range(SIDE)])
    row_b = jnp.stack([turn(part_b, "z", k) for k in range(SIDE)])
    blocks = [turn(row_a, "z", m) for m in range(SIDE)] + [turn(row_b, "x", m) for m in range(SIDE)]

    asked = [
        turn(lax.dynamic_slice_in_dim(queries, lax.rem(y + r, SIDE) * head_cols, head_cols, 1), "y", r)
        for r in range(SIDE)
    ]

    by_stream = streams.transpose(1, 0, 2)
    route = [(i, i + 1) for i in range(SIDE**3 - 1)]
    halo = lax.ppermute(by_stream[:, ROWS - SUB:], ctx, route).astype(jnp.float32)
    rate = rates.reshape(MODES, width // LANES, LANES)
    decay = jnp.exp(-rate)
    weight = residues.reshape(MODES, width // LANES, LANES) * jnp.sqrt(-jnp.expm1(-2.0 * rate))
    base, first, end = mixer(by_stream, halo, short_taps.transpose(1, 0, 2), decay, weight, residual)

    def level(value, axis, place, span, last):
        sent = value.astype(jnp.bfloat16)
        others = [turn(sent, axis, k).astype(jnp.float32) for k in range(1, SIDE)]
        before = jnp.zeros_like(value)
        total = value * jnp.exp(-rate * (span * (SIDE - 1 - place)).astype(jnp.float32))
        for k, other in enumerate(others, 1):
            kept = jnp.exp(-rate * float(span * (k - 1)))
            before = before + jnp.where(place >= k, kept * other, 0.0)
            origin = lax.rem(place - k + SIDE, SIDE)
            total = total + other * jnp.exp(-rate * (span * (SIDE - 1 - origin)).astype(jnp.float32))
        return before, total

    before_x, total_x = level(end, "x", x, ROWS, False)
    before_z, total_z = level(total_x, "z", z, ROWS * SIDE, False)
    before_y, _ = level(total_z, "y", y, ROWS * SIDE * SIDE, True)
    entering = (
        before_x
        + jnp.exp(-rate * (ROWS * x).astype(jnp.float32)) * before_z
        + jnp.exp(-rate * (ROWS * (SIDE * z + x)).astype(jnp.float32)) * before_y
    )
    base = carried(entering, decay, weight, base, first)

    parts = {}
    for r in (2, 1, 3, 0):
        place = jnp.stack([y, z, x, jnp.int32(r)])
        parts[r] = turn(attend(place, lengths, asked[r], blocks), "y", SIDE - r)
    attended = jnp.zeros(residual.shape, jnp.bfloat16)
    for r in range(SIDE):
        attended = lax.dynamic_update_slice_in_dim(attended, parts[r], lax.rem(y + r, SIDE) * head_cols, 1)

    stream = (base + attended.astype(jnp.float32)).astype(jnp.bfloat16)
    wide = stream.astype(jnp.float32)
    squares = lax.psum(jnp.sum(wide * wide, axis=1), "tp")
    mean_square = squares / (width * lax.axis_size("tp"))
    normed = (wide * lax.rsqrt(mean_square[:, None] + 1e-06) * gain).astype(jnp.bfloat16)
    return (stream, normed, attended)


def solution(mesh):
    split = Mesh(mesh.devices.reshape(SIDE, SIDE, SIDE, 2), ("y", "z", "x", "tp"))
    ctx = ("y", "z", "x")
    in_specs = (
        P(ctx, None, "tp"),
        P(None, None, "tp"),
        P(None, "tp"),
        P(None, "tp"),
        P(ctx, "tp"),
        P("tp"),
        P(ctx, "tp"),
        P(ctx, None, "tp"),
        P(),
    )
    out_specs = (P(ctx, "tp"), P(ctx, "tp"), P(ctx, "tp"))
    return jax.shard_map(local, mesh=split, in_specs=in_specs, out_specs=out_specs, check_vma=False)
```

time: 738 us -> 191 us (0.26)
  the two profiles are of different devices: /device:TPU:127 before, /device:TPU:115 now
where the time goes in v1:
time: 191 us; the launch traced here: 193 us
  Pallas kernels  72.2 us (38%)
  starting transfers between devices  59.3 us (31%)
  waiting for transfers between devices  23.4 us (12%)
  local copies, waits for them, and re-layouts  20.2 us (11%)
  other arithmetic  12.7 us (7%)
  blocking collectives  3.64 us (2%)
    ppermute x30, starting transfers between devices, turn(): lax.ppermute(value, axis, [(i, (i + distance) % SIDE) for i in range(SIDE)])  56.2 us
    pallas_call x4, Pallas kernels, attend(): pl.pallas_call(attend_kernel, in_specs=[smem, smem, vmem] + [pl.BlockSpec...  47.9 us
    ppermute x30, waiting for transfers between devices, turn(): lax.ppermute(value, axis, [(i, (i + distance) % SIDE) for i in range(SIDE)])  23.4 us
    pallas_call x1, Pallas kernels, mixer(): pl.pallas_call(mixer_kernel, grid=(steps,), in_specs=[pl.BlockSpec((3, RO...  18.5 us
    unnamed x112, local copies, waits for them, and re-layouts  16.7 us
    pallas_call x1, Pallas kernels, carried(): pl.pallas_call(carried_kernel, grid=(steps,), in_specs=[modes, modes, mod...  5.87 us
  transfers between devices with their start and end apart: 31, of which 7 were waited for; matrix products, arithmetic and copies ran while one was open for 13% of the time, Pallas kernels for 37%

profile of v1, /device:TPU:115, one launch (start us, length us, event | category | flops | bytes accessed | tf_op | source)
XLA Modules:
  0.0 193.0 jit_solution(11693504002533142408)
XLA Ops:
  0.6 1.7 slice.4
  2.3 3.1 %collective-permute-start = (bf16[3,8,4096]{2,1,0:T(8,128)(2,1)}, bf16[3,8,4096]{2,1,0:T(8,128)(2,1)}, u32[]{:S(2)}, u32[]{:S(2)}) collective-permute-start(bf16[3,8,4096]{2,1,0:T(8,128)(2,1)} %slice.4), channel_id=1, source_target_pairs={{0,2},{2,4},{4,6},{6,8},{8,10},{10,12},{12,14},{14,16},{16,18},{18... | collective-permute-start | bytes 589832 | tf_op jit(solution)/shard_map/ppermute | solution.py:271
  5.4 1.2 copy.12
  6.6 0.7 constant_dynamic-slice_fusion.4
  7.3 0.7 copy.18
  8.0 1.0 collective-permute-start.10
  9.0 0.7 copy.20
  9.8 0.5 collective-permute-start.18
  10.2 3.2 %exponential_bitcast_fusion.5 = (f32[2,8,32,128]{3,1,2,0:T(8,128)}, f32[2,8,32,128]{3,1,2,0:T(8,128)S(1)}, f32[2,8,32,128]{3,1,2,0:T(8,128)}, f32[2,8,32,128]{3,...) fusion(f32[]{:T(128)S(6)} %convert_element_type.96, ...), kind=kLoop, calls=%fused_computation.57 | loop fusion | flops 1376256 | bytes 5505064
  13.5 0.8 copy.23
  14.3 1.0 convert_element_type.81.halo_ref
  15.3 0.9 copy-done.1
  16.2 1.2 copy-done.7
  17.5 1.0 copy-done.10
  18.4 18.5 %mixer.1 = (f32[128,4096]{1,0:T(8,128)S(1)}, f32[128,4096]{1,0:T(8,128)S(1)}, f32[16,32,128]{2,1,0:T(8,128)S(1)}) custom-call(bf16[3,128,4096]{2,1,0:T(8,128)(2,1)S(1)} %bitcast.131, f32[3,8,4096]{2,1,0:T(8,128)S(1)} %convert_element_type.81.halo_ref, f32[3,7,4096]{2,1,0:T(8,128)S(1)} %bitcast.136, f32[16,32,128]{2,1,0:T(8,128)S(1)} %bitcast.132, ...), custom_call_target="tpu_custom_call" | custom-call | flops 80000000 | bytes 10000000 | tf_op jit(solution)/shard_map/mixer/pallas_call | solution.py:181
  37.0 0.7 convert_element_type.82
  37.7 0.9 collective-permute-start.1
  38.6 1.1 collective-permute-start.2
  39.7 0.7 collective-permute-start.3
  40.4 1.0 constant_dynamic-slice_fusion
  41.8 0.5 copy-done.20
  42.4 1.0 copy.17
  43.4 1.6 copy.19
  45.0 1.3 collective-permute-start.17
  46.3 0.9 fusion.30
  47.2 2.1 %collective-permute-start.13 = (bf16[2,2,128,128]{3,2,1,0:T(8,128)(2,1)S(1)}, bf16[2,2,128,128]{3,2,1,0:T(8,128)(2,1)S(1)}, u32[]{:S(2)}, u32[]{:S(2)}) collective-permute-start(bf16[2,2,128,128]{3,2,1,0:T(8,128)(2,1)S(1)} %get-tuple-element.45), channel_id=1, source_target_pairs={{0,6},{2,0},{4,2},{6,4},{1,7},{3,1},{5,3},{7,5},{8,14},{10,8},{12,... | collective-permute-start | bytes 393224 | tf_op jit(solution)/shard_map/ppermute | solution.py:27
  49.3 1.3 collective-permute-start.11
  50.6 1.0 fusion.31
  51.8 4.3 %collective-permute-done.12 = bf16[2,2,128,128]{3,2,1,0:T(8,128)(2,1)S(1)} collective-permute-done((bf16[2,2,128,128]{3,2,1,0:T(8,128)(2,1)S(1)}, bf16[2,2,128,128]{3,2,1,0:T(8,128)(2,1)S(1)}, u32[]{:S(2)}, u32[]{:S(2)}) %collective-permute-start.12) | collective-permute-done | bytes 131104 | tf_op jit(solution)/shard_map/ppermute | solution.py:27
  56.5 0.6 collective-permute-start.25
  57.1 2.7 %collective-permute-start.14 = (bf16[4,2,2,128,128]{4,3,2,1,0:T(8,128)(2,1)S(1)}, bf16[4,2,2,128,128]{4,3,2,1,0:T(8,128)(2,1)S(1)}, u32[]{:S(2)}, u32[]{:S(2)}) collective-permute-start(bf16[4,2,2,128,128]{4,3,2,1,0:T(8,128)(2,1)S(1)} %pad_maximum_fusion.a0), channel_id=1, source_target_pairs={{0,8},{8,16},{16,24},{24,0},{1,9},{9,17},{17,25},{25,1},{2,10},{10... | collective-permute-start | bytes 1572872 | tf_op jit(solution)/shard_map/ppermute | solution.py:27
  59.8 1.5 fusion.29
  61.5 2.0 %collective-permute-start.20 = (bf16[2,2,128,128]{3,2,1,0:T(8,128)(2,1)S(1)}, bf16[2,2,128,128]{3,2,1,0:T(8,128)(2,1)S(1)}, u32[]{:S(2)}, u32[]{:S(2)}) collective-permute-start(bf16[2,2,128,128]{3,2,1,0:T(8,128)(2,1)S(1)} %get-tuple-element.43), channel_id=1, source_target_pairs={{0,16},{8,24},{16,0},{24,8},{1,17},{9,25},{17,1},{25,9},{2,18},{10... | collective-permute-start | bytes 393224 | tf_op jit(solution)/shard_map/ppermute | solution.py:27
  63.5 1.5 collective-permute-start.19
  65.0 0.8 fusion.20
  65.9 1.4 collective-permute-done.21
  67.2 0.9 collective-permute-start.9
  68.2 0.5 collective-permute-done.20
  68.7 2.7 %collective-permute-start.8 = (bf16[16,32,128]{2,1,0:T(8,128)(2,1)}, bf16[16,32,128]{2,1,0:T(8,128)(2,1)}, u32[]{:S(2)}, u32[]{:S(2)}) collective-permute-start(bf16[16,32,128]{2,1,0:T(8,128)(2,1)} %fusion.20), channel_id=1, source_target_pairs={{0,64},{32,96},{64,0},{96,32},{1,65},{33,97},{65,1},{97,33},{2,66}... | collective-permute-start | bytes 393224 | tf_op jit(solution)/shard_map/ppermute | solution.py:27
  71.4 4.3 %collective-permute-done.19 = bf16[2,2,128,128]{3,2,1,0:T(8,128)(2,1)S(1)} collective-permute-done((bf16[2,2,128,128]{3,2,1,0:T(8,128)(2,1)S(1)}, bf16[2,2,128,128]{3,2,1,0:T(8,128)(2,1)S(1)}, u32[]{:S(2)}, u32[]{:S(2)}) %collective-permute-start.19) | collective-permute-done | bytes 131104 | tf_op jit(solution)/shard_map/ppermute | solution.py:27
  75.7 0.6 copy-done.41
  76.4 1.0 copy.39
  77.5 1.1 copy.38
  78.6 1.0 copy.33
  79.6 1.1 copy.32
  80.7 1.0 copy.31
  82.1 3.8 %collective-permute-start.15 = (bf16[4,2,2,128,128]{4,3,2,1,0:T(8,128)(2,1)S(1)}, bf16[4,2,2,128,128]{4,3,2,1,0:T(8,128)(2,1)S(1)}, u32[]{:S(2)}, u32[]{:S(2)}) collective-permute-start(bf16[4,2,2,128,128]{4,3,2,1,0:T(8,128)(2,1)S(1)} %pad_maximum_fusion.a0), channel_id=1, source_target_pairs={{0,16},{8,24},{16,0},{24,8},{1,17},{9,25},{17,1},{25,9},{2,18},{10... | collective-permute-start | bytes 1572872 | tf_op jit(solution)/shard_map/ppermute | solution.py:27
  86.1 1.0 collective-permute-start.23
  87.1 0.8 collective-permute-start.24
  88.0 1.6 fusion.7.state_ref
  89.6 5.9 %carried.1 = f32[128,4096]{1,0:T(8,128)S(1)} custom-call(f32[16,32,128]{2,1,0:T(8,128)S(1)} %fusion.7.state_ref, f32[16,32,128]{2,1,0:T(8,128)S(1)} %bitcast.133, f32[16,32,128]{2,1,0:T(8,128)S(1)} %bitcast.135, f32[128,4096]{1,0:T(8,128)S(1)} %copy-done.4, f32[128,4096]{1,0:T(8,128)S(1)} %copy-done.6), custom_call_target="tpu_custom_call" | custom-call | flops 20000000 | bytes 6000000 | tf_op jit(solution)/shard_map/carried/pallas_call | solution.py:214
  95.5 2.1 %collective-permute-start.27 = (bf16[128,1024]{1,0:T(8,128)(2,1)S(1)}, bf16[128,1024]{1,0:T(8,128)(2,1)S(1)}, u32[]{:S(2)}, u32[]{:S(2)}) collective-permute-start(bf16[128,1024]{1,0:T(8,128)(2,1)S(1)} %copy-done.35), channel_id=1, source_target_pairs={{0,64},{32,96},{64,0},{96,32},{1,65},{33,97},{65,1},{97,33},{2,66}... | collective-permute-start | bytes 786440 | tf_op jit(solution)/shard_map/ppermute | solution.py:27
  97.6 11.9 %collective-permute-done.16.a3 = bf16[4,2,2,128,128]{4,3,2,1,0:T(8,128)(2,1)S(1)} collective-permute-done((bf16[4,2,2,128,128]{4,3,2,1,0:T(8,128)(2,1)S(1)}, bf16[4,2,2,128,128]{4,3,2,1,0:T(8,128)(2,1)S(1)}, u32[]{:S(2)}, u32[]{:S(2)}) %collective-permute-start.16) | collective-permute-done | bytes 524320 | tf_op jit(solution)/shard_map/ppermute | solution.py:27
  109.6 1.0 collective-permute-start.29
  110.6 0.7 collective-permute-done.24.b3
  111.3 11.3 %attend.5 = bf16[128,1024]{1,0:T(8,128)(2,1)S(1)} custom-call(s32[4]{0:T(128)S(1)} %get-tuple-element.47.place_ref, s32[4]{0:T(128)S(1)} %copy-done.11, bf16[128,1024]{1,0:T(8,128)(2,1)S(1)} %collective-permute-done.25.q_ref, bf16[4,2,2,128,128]{4,3,2,1,0:T(8,128)(2,1)S(1)} %pad_maximum_fusion.a0, ...), custom_call_target="tpu_custom_call" | custom-call | flops 3000000000 | bytes 2000000 | tf_op jit(solution)/shard_map/attend/pallas_call | solution.py:230
  122.7 5.3 %attend.6 = bf16[128,1024]{1,0:T(8,128)(2,1)S(1)} custom-call(s32[4]{0:T(128)S(1)} %get-tuple-element.46.place_ref, s32[4]{0:T(128)S(1)} %copy-done.11, bf16[128,1024]{1,0:T(8,128)(2,1)S(1)} %collective-permute-done.27.q_ref, bf16[4,2,2,128,128]{4,3,2,1,0:T(8,128)(2,1)S(1)} %pad_maximum_fusion.a0, ...), custom_call_target="tpu_custom_call" | custom-call | flops 3000000000 | bytes 2000000 | tf_op jit(solution)/shard_map/attend/pallas_call | solution.py:230
  128.1 27.4 %collective-permute-start.28 = (bf16[128,1024]{1,0:T(8,128)(2,1)S(1)}, bf16[128,1024]{1,0:T(8,128)(2,1)S(1)}, u32[]{:S(2)}, u32[]{:S(2)}) collective-permute-start(bf16[128,1024]{1,0:T(8,128)(2,1)S(1)} %attend.6), channel_id=1, source_target_pairs={{0,64},{32,96},{64,0},{96,32},{1,65},{33,97},{65,1},{97,33},{2,66}... | collective-permute-start | bytes 786440 | tf_op jit(solution)/shard_map/ppermute | solution.py:27
  155.5 11.3 %attend.7 = bf16[128,1024]{1,0:T(8,128)(2,1)S(1)} custom-call(s32[4]{0:T(128)S(1)} %get-tuple-element.11.place_ref, s32[4]{0:T(128)S(1)} %copy-done.11, bf16[128,1024]{1,0:T(8,128)(2,1)S(1)} %collective-permute-done.29.q_ref, bf16[4,2,2,128,128]{4,3,2,1,0:T(8,128)(2,1)S(1)} %pad_maximum_fusion.a0, ...), custom_call_target="tpu_custom_call" | custom-call | flops 3000000000 | bytes 2000000 | tf_op jit(solution)/shard_map/attend/pallas_call | solution.py:230
  166.9 19.9 %attend.4 = bf16[128,1024]{1,0:T(8,128)(2,1)S(1)} custom-call(s32[4]{0:T(128)S(1)} %get-tuple-element.48.place_ref, s32[4]{0:T(128)S(1)} %copy-done.11, bf16[128,1024]{1,0:T(8,128)(2,1)S(1)} %get-tuple-element.17.q_ref, bf16[4,2,2,128,128]{4,3,2,1,0:T(8,128)(2,1)S(1)} %pad_maximum_fusion.a0, bf16[4,2,2,128,128]{4,3,2,1,0:T(8,128)(2,1)S(1)} %collective-permute-done.14.a1, ...), custom_call_target="tpu_custom_call" | custom-call | flops 3000000000 | bytes 2000000 | tf_op jit(solution)/shard_map/attend/pallas_call | solution.py:230
  187.0 0.4 fusion
  187.5 0.5 copy-done.13
  188.0 3.6 %psum.7 = f32[128]{0:T(128)S(1)} all-reduce(f32[128]{0:T(128)S(1)} %get-tuple-element.9), channel_id=1, replica_groups=mesh['y'=4,'z'=4,'x'=4,'tp'=2] {'tp'}, use_global_device_ids=true, to_apply=%region_1.2 | all-reduce | flops 128 | bytes 1024 | tf_op jit(solution)/shard_map/psum | solution.py:309
  191.7 1.3 fusion.2
  (140 shorter events, 2.3 us)
Async XLA Ops:
  0.6 9.6 %copy-start.36 = (f32[16,4096]{1,0:T(8,128)S(1)}, f32[16,4096]{1,0:T(8,128)}, u32[]{:S(2)}) copy-start(f32[16,4096]{1,0:T(8,128)} %param.11) | copy-start | bytes 786436
  2.3 12.0 %collective-permute-start = (bf16[3,8,4096]{2,1,0:T(8,128)(2,1)}, bf16[3,8,4096]{2,1,0:T(8,128)(2,1)}, u32[]{:S(2)}, u32[]{:S(2)}) collective-permute-start(bf16[3,8,4096]{2,1,0:T(8,128)(2,1)} %slice.4), channel_id=1, source_target_pairs={{0,2},{2,4},{4,6},{6,8},{8,10},{10,12},{12,14},{14,16},{16,18},{18... | collective-permute-start | bytes 589832 | tf_op jit(solution)/shard_map/ppermute | solution.py:271
  8.0 36.9 %collective-permute-start.10 = (bf16[2,128,128]{2,1,0:T(8,128)(2,1)}, bf16[2,128,128]{2,1,0:T(8,128)(2,1)}, u32[]{:S(2)}, u32[]{:S(2)}) collective-permute-start(bf16[2,128,128]{2,1,0:T(8,128)(2,1)} %bitcast.8), channel_id=1, source_target_pairs={{0,32},{32,64},{64,96},{96,0},{1,33},{33,65},{65,97},{97,1},{2,34}... | collective-permute-start | bytes 196616 | tf_op jit(solution)/shard_map/ppermute | solution.py:27
  9.8 46.7 %collective-permute-start.18 = (bf16[2,128,128]{2,1,0:T(8,128)(2,1)}, bf16[2,128,128]{2,1,0:T(8,128)(2,1)}, u32[]{:S(2)}, u32[]{:S(2)}) collective-permute-start(bf16[2,128,128]{2,1,0:T(8,128)(2,1)} %bitcast.18), channel_id=1, source_target_pairs={{0,96},{32,0},{64,32},{96,64},{1,97},{33,1},{65,33},{97,65},{2,98}... | collective-permute-start | bytes 196616 | tf_op jit(solution)/shard_map/ppermute | solution.py:27
  10.2 5.0 %copy-start = (bf16[128,3,4096]{2,0,1:T(8,128)(2,1)S(1)}, bf16[128,3,4096]{2,0,1:T(8,128)(2,1)}, u32[]{:S(2)}) copy-start(bf16[128,3,4096]{2,0,1:T(8,128)(2,1)} %param.9) | copy-start | bytes 9437188
  18.4 22.0 %copy-start.14 = (bf16[128,4096]{1,0:T(8,128)(2,1)S(1)}, bf16[128,4096]{1,0:T(8,128)(2,1)}, u32[]{:S(2)}) copy-start(bf16[128,4096]{1,0:T(8,128)(2,1)} %param.15) | copy-start | bytes 3145732
  36.9 4.7 %copy-start.3 = (f32[128,4096]{1,0:T(8,128)}, f32[128,4096]{1,0:T(8,128)S(1)}, u32[]{:S(2)}) copy-start(f32[128,4096]{1,0:T(8,128)S(1)} %get-tuple-element.7.base_ref) | copy-start | bytes 6291460
  37.0 4.7 %copy-start.5 = (f32[128,4096]{1,0:T(8,128)}, f32[128,4096]{1,0:T(8,128)S(1)}, u32[]{:S(2)}) copy-start(f32[128,4096]{1,0:T(8,128)S(1)} %get-tuple-element.8.first_ref) | copy-start | bytes 6291460
  37.0 4.7 %copy-start.8 = (f32[16,32,128]{2,1,0:T(8,128)}, f32[16,32,128]{2,1,0:T(8,128)S(1)}, u32[]{:S(2)}) copy-start(f32[16,32,128]{2,1,0:T(8,128)S(1)} %get-tuple-element.6) | copy-start | bytes 786436
  37.0 4.4 %copy-start.25 = (f32[2,8,32,128]{3,1,2,0:T(8,128)S(1)}, f32[2,8,32,128]{3,1,2,0:T(8,128)}, u32[]{:S(2)}) copy-start(f32[2,8,32,128]{3,1,2,0:T(8,128)} %get-tuple-element.30) | copy-start | bytes 786436
  37.0 4.5 %copy-start.24 = (f32[2,8,32,128]{3,1,2,0:T(8,128)S(1)}, f32[2,8,32,128]{3,1,2,0:T(8,128)}, u32[]{:S(2)}) copy-start(f32[2,8,32,128]{3,1,2,0:T(8,128)} %get-tuple-element.29) | copy-start | bytes 786436
  37.0 4.6 %copy-start.23 = (f32[2,8,32,128]{3,1,2,0:T(8,128)S(1)}, f32[2,8,32,128]{3,1,2,0:T(8,128)}, u32[]{:S(2)}) copy-start(f32[2,8,32,128]{3,1,2,0:T(8,128)} %get-tuple-element.28) | copy-start | bytes 786436
  37.7 9.5 %collective-permute-start.1 = (bf16[16,32,128]{2,1,0:T(8,128)(2,1)}, bf16[16,32,128]{2,1,0:T(8,128)(2,1)S(1)}, u32[]{:S(2)}, u32[]{:S(2)}) collective-permute-start(bf16[16,32,128]{2,1,0:T(8,128)(2,1)} %convert_element_type.82), channel_id=1, source_target_pairs={{0,2},{2,4},{4,6},{6,0},{1,3},{3,5},{5,7},{7,1},{8,10},{10,12},{12... | collective-permute-start | bytes 393224 | tf_op jit(solution)/shard_map/ppermute | solution.py:27
  38.6 10.7 %collective-permute-start.2 = (bf16[16,32,128]{2,1,0:T(8,128)(2,1)}, bf16[16,32,128]{2,1,0:T(8,128)(2,1)S(1)}, u32[]{:S(2)}, u32[]{:S(2)}) collective-permute-start(bf16[16,32,128]{2,1,0:T(8,128)(2,1)} %convert_element_type.82), channel_id=1, source_target_pairs={{0,4},{2,6},{4,0},{6,2},{1,5},{3,7},{5,1},{7,3},{8,12},{10,14},{12... | collective-permute-start | bytes 393224 | tf_op jit(solution)/shard_map/ppermute | solution.py:27
  39.7 9.6 %collective-permute-start.3 = (bf16[16,32,128]{2,1,0:T(8,128)(2,1)}, bf16[16,32,128]{2,1,0:T(8,128)(2,1)}, u32[]{:S(2)}, u32[]{:S(2)}) collective-permute-start(bf16[16,32,128]{2,1,0:T(8,128)(2,1)} %convert_element_type.82), channel_id=1, source_target_pairs={{0,6},{2,0},{4,2},{6,4},{1,7},{3,1},{5,3},{7,5},{8,14},{10,8},{12,... | collective-permute-start | bytes 393224 | tf_op jit(solution)/shard_map/ppermute | solution.py:27
  41.7 8.9 %copy-start.9 = (f32[16,32,128]{2,1,0:T(8,128)S(1)}, f32[16,32,128]{2,1,0:T(8,128)}, u32[]{:S(2)}) copy-start(f32[16,32,128]{2,1,0:T(8,128)} %copy-done.8) | copy-start | bytes 786436
  45.0 12.1 %collective-permute-start.17 = (bf16[2,128,128]{2,1,0:T(8,128)(2,1)}, bf16[2,128,128]{2,1,0:T(8,128)(2,1)S(1)}, u32[]{:S(2)}, u32[]{:S(2)}) collective-permute-start(bf16[2,128,128]{2,1,0:T(8,128)(2,1)} %bitcast.15), channel_id=1, source_target_pairs={{0,64},{32,96},{64,0},{96,32},{1,65},{33,97},{65,1},{97,33},{2,66}... | collective-permute-start | bytes 196616 | tf_op jit(solution)/shard_map/ppermute | solution.py:27
  47.2 4.5 %copy-start.29 = (bf16[16,32,128]{2,1,0:T(8,128)(2,1)}, bf16[16,32,128]{2,1,0:T(8,128)(2,1)S(1)}, u32[]{:S(2)}) copy-start(bf16[16,32,128]{2,1,0:T(8,128)(2,1)S(1)} %collective-permute-done.1) | copy-start | bytes 393220
  47.2 4.5 %collective-permute-start.13 = (bf16[2,2,128,128]{3,2,1,0:T(8,128)(2,1)S(1)}, bf16[2,2,128,128]{3,2,1,0:T(8,128)(2,1)S(1)}, u32[]{:S(2)}, u32[]{:S(2)}) collective-permute-start(bf16[2,2,128,128]{3,2,1,0:T(8,128)(2,1)S(1)} %get-tuple-element.45), channel_id=1, source_target_pairs={{0,6},{2,0},{4,2},{6,4},{1,7},{3,1},{5,3},{7,5},{8,14},{10,8},{12,... | collective-permute-start | bytes 393224 | tf_op jit(solution)/shard_map/ppermute | solution.py:27
  49.3 6.7 %collective-permute-start.12 = (bf16[2,2,128,128]{3,2,1,0:T(8,128)(2,1)S(1)}, bf16[2,2,128,128]{3,2,1,0:T(8,128)(2,1)S(1)}, u32[]{:S(2)}, u32[]{:S(2)}) collective-permute-start(bf16[2,2,128,128]{3,2,1,0:T(8,128)(2,1)S(1)} %get-tuple-element.45), channel_id=1, source_target_pairs={{0,4},{2,6},{4,0},{6,2},{1,5},{3,7},{5,1},{7,3},{8,12},{10,14},{12... | collective-permute-start | bytes 393224 | tf_op jit(solution)/shard_map/ppermute | solution.py:27
  49.3 7.1 %collective-permute-start.11 = (bf16[2,2,128,128]{3,2,1,0:T(8,128)(2,1)S(1)}, bf16[2,2,128,128]{3,2,1,0:T(8,128)(2,1)S(1)}, u32[]{:S(2)}, u32[]{:S(2)}) collective-permute-start(bf16[2,2,128,128]{3,2,1,0:T(8,128)(2,1)S(1)} %get-tuple-element.45), channel_id=1, source_target_pairs={{0,2},{2,4},{4,6},{6,0},{1,3},{3,5},{5,7},{7,1},{8,10},{10,12},{12... | collective-permute-start | bytes 393224 | tf_op jit(solution)/shard_map/ppermute | solution.py:27
  51.7 9.6 %collective-permute-start.4 = (bf16[16,32,128]{2,1,0:T(8,128)(2,1)S(1)}, bf16[16,32,128]{2,1,0:T(8,128)(2,1)S(1)}, u32[]{:S(2)}, u32[]{:S(2)}) collective-permute-start(bf16[16,32,128]{2,1,0:T(8,128)(2,1)S(1)} %get-tuple-element.13), channel_id=1, source_target_pairs={{0,8},{8,16},{16,24},{24,0},{1,9},{9,17},{17,25},{25,1},{2,10},{10... | collective-permute-start | bytes 393224 | tf_op jit(solution)/shard_map/ppermute | solution.py:27
  56.0 5.4 %collective-permute-start.5 = (bf16[16,32,128]{2,1,0:T(8,128)(2,1)S(1)}, bf16[16,32,128]{2,1,0:T(8,128)(2,1)S(1)}, u32[]{:S(2)}, u32[]{:S(2)}) collective-permute-start(bf16[16,32,128]{2,1,0:T(8,128)(2,1)S(1)} %get-tuple-element.13), channel_id=1, source_target_pairs={{0,16},{8,24},{16,0},{24,8},{1,17},{9,25},{17,1},{25,9},{2,18},{10... | collective-permute-start | bytes 393224 | tf_op jit(solution)/shard_map/ppermute | solution.py:27
  56.4 7.1 %collective-permute-start.6 = (bf16[16,32,128]{2,1,0:T(8,128)(2,1)S(1)}, bf16[16,32,128]{2,1,0:T(8,128)(2,1)S(1)}, u32[]{:S(2)}, u32[]{:S(2)}) collective-permute-start(bf16[16,32,128]{2,1,0:T(8,128)(2,1)S(1)} %get-tuple-element.13), channel_id=1, source_target_pairs={{0,24},{8,0},{16,8},{24,16},{1,25},{9,1},{17,9},{25,17},{2,26},{10... | collective-permute-start | bytes 393224 | tf_op jit(solution)/shard_map/ppermute | solution.py:27
  56.5 25.6 %collective-permute-start.25 = (bf16[128,1024]{1,0:T(8,128)(2,1)}, bf16[128,1024]{1,0:T(8,128)(2,1)S(1)}, u32[]{:S(2)}, u32[]{:S(2)}) collective-permute-start(bf16[128,1024]{1,0:T(8,128)(2,1)} %get-tuple-element.16), channel_id=1, source_target_pairs={{0,32},{32,64},{64,96},{96,0},{1,33},{33,65},{65,97},{97,1},{2,34}... | collective-permute-start | bytes 786440 | tf_op jit(solution)/shard_map/ppermute | solution.py:27
  57.1 30.0 %collective-permute-start.14 = (bf16[4,2,2,128,128]{4,3,2,1,0:T(8,128)(2,1)S(1)}, bf16[4,2,2,128,128]{4,3,2,1,0:T(8,128)(2,1)S(1)}, u32[]{:S(2)}, u32[]{:S(2)}) collective-permute-start(bf16[4,2,2,128,128]{4,3,2,1,0:T(8,128)(2,1)S(1)} %pad_maximum_fusion.a0), channel_id=1, source_target_pairs={{0,8},{8,16},{16,24},{24,0},{1,9},{9,17},{17,25},{25,1},{2,10},{10... | collective-permute-start | bytes 1572872 | tf_op jit(solution)/shard_map/ppermute | solution.py:27
  61.3 6.0 %collective-permute-start.21 = (bf16[2,2,128,128]{3,2,1,0:T(8,128)(2,1)S(1)}, bf16[2,2,128,128]{3,2,1,0:T(8,128)(2,1)S(1)}, u32[]{:S(2)}, u32[]{:S(2)}) collective-permute-start(bf16[2,2,128,128]{3,2,1,0:T(8,128)(2,1)S(1)} %get-tuple-element.43), channel_id=1, source_target_pairs={{0,24},{8,0},{16,8},{24,16},{1,25},{9,1},{17,9},{25,17},{2,26},{10... | collective-permute-start | bytes 393224 | tf_op jit(solution)/shard_map/ppermute | solution.py:27
  61.5 7.2 %collective-permute-start.20 = (bf16[2,2,128,128]{3,2,1,0:T(8,128)(2,1)S(1)}, bf16[2,2,128,128]{3,2,1,0:T(8,128)(2,1)S(1)}, u32[]{:S(2)}, u32[]{:S(2)}) collective-permute-start(bf16[2,2,128,128]{3,2,1,0:T(8,128)(2,1)S(1)} %get-tuple-element.43), channel_id=1, source_target_pairs={{0,16},{8,24},{16,0},{24,8},{1,17},{9,25},{17,1},{25,9},{2,18},{10... | collective-permute-start | bytes 393224 | tf_op jit(solution)/shard_map/ppermute | solution.py:27
  63.5 12.2 %copy-start.27 = (bf16[16,32,128]{2,1,0:T(8,128)(2,1)}, bf16[16,32,128]{2,1,0:T(8,128)(2,1)S(1)}, u32[]{:S(2)}) copy-start(bf16[16,32,128]{2,1,0:T(8,128)(2,1)S(1)} %collective-permute-done.6) | copy-start | bytes 393220
  63.5 12.2 %collective-permute-start.19 = (bf16[2,2,128,128]{3,2,1,0:T(8,128)(2,1)S(1)}, bf16[2,2,128,128]{3,2,1,0:T(8,128)(2,1)S(1)}, u32[]{:S(2)}, u32[]{:S(2)}) collective-permute-start(bf16[2,2,128,128]{3,2,1,0:T(8,128)(2,1)S(1)} %get-tuple-element.43), channel_id=1, source_target_pairs={{0,8},{8,16},{16,24},{24,0},{1,9},{9,17},{17,25},{25,1},{2,10},{10... | collective-permute-start | bytes 393224 | tf_op jit(solution)/shard_map/ppermute | solution.py:27
  65.9 15.8 %copy-start.18 = (f32[2,8,32,128]{3,1,2,0:T(8,128)S(1)}, f32[2,8,32,128]{3,1,2,0:T(8,128)}, u32[]{:S(2)}) copy-start(f32[2,8,32,128]{3,1,2,0:T(8,128)} %get-tuple-element.27) | copy-start | bytes 786436
  65.9 15.9 %copy-start.17 = (f32[2,8,32,128]{3,1,2,0:T(8,128)S(1)}, f32[2,8,32,128]{3,1,2,0:T(8,128)}, u32[]{:S(2)}) copy-start(f32[2,8,32,128]{3,1,2,0:T(8,128)} %get-tuple-element.26) | copy-start | bytes 786436
  65.9 16.0 %copy-start.16 = (f32[2,8,32,128]{3,1,2,0:T(8,128)S(1)}, f32[2,8,32,128]{3,1,2,0:T(8,128)}, u32[]{:S(2)}) copy-start(f32[2,8,32,128]{3,1,2,0:T(8,128)} %get-tuple-element.25) | copy-start | bytes 786436
  67.2 8.5 %copy-start.37 = (bf16[2,2,128,128]{3,2,1,0:T(8,128)(2,1)}, bf16[2,2,128,128]{3,2,1,0:T(8,128)(2,1)S(1)}, u32[]{:S(2)}) copy-start(bf16[2,2,128,128]{3,2,1,0:T(8,128)(2,1)S(1)} %collective-permute-done.21) | copy-start | bytes 393220
  67.2 18.7 %collective-permute-start.9 = (bf16[16,32,128]{2,1,0:T(8,128)(2,1)}, bf16[16,32,128]{2,1,0:T(8,128)(2,1)}, u32[]{:S(2)}, u32[]{:S(2)}) collective-permute-start(bf16[16,32,128]{2,1,0:T(8,128)(2,1)} %fusion.20), channel_id=1, source_target_pairs={{0,96},{32,0},{64,32},{96,64},{1,97},{33,1},{65,33},{97,65},{2,98}... | collective-permute-start | bytes 393224 | tf_op jit(solution)/shard_map/ppermute | solution.py:27
  68.6 7.1 %copy-start.39 = (bf16[2,2,128,128]{3,2,1,0:T(8,128)(2,1)}, bf16[2,2,128,128]{3,2,1,0:T(8,128)(2,1)S(1)}, u32[]{:S(2)}) copy-start(bf16[2,2,128,128]{3,2,1,0:T(8,128)(2,1)S(1)} %collective-permute-done.20) | copy-start | bytes 393220
  68.7 17.3 %collective-permute-start.8 = (bf16[16,32,128]{2,1,0:T(8,128)(2,1)}, bf16[16,32,128]{2,1,0:T(8,128)(2,1)}, u32[]{:S(2)}, u32[]{:S(2)}) collective-permute-start(bf16[16,32,128]{2,1,0:T(8,128)(2,1)} %fusion.20), channel_id=1, source_target_pairs={{0,64},{32,96},{64,0},{96,32},{1,65},{33,97},{65,1},{97,33},{2,66}... | collective-permute-start | bytes 393224 | tf_op jit(solution)/shard_map/ppermute | solution.py:27
  75.7 10.3 %collective-permute-start.7 = (bf16[16,32,128]{2,1,0:T(8,128)(2,1)}, bf16[16,32,128]{2,1,0:T(8,128)(2,1)}, u32[]{:S(2)}, u32[]{:S(2)}) collective-permute-start(bf16[16,32,128]{2,1,0:T(8,128)(2,1)} %fusion.20), channel_id=1, source_target_pairs={{0,32},{32,64},{64,96},{96,0},{1,33},{33,65},{65,97},{97,1},{2,34}... | collective-permute-start | bytes 393224 | tf_op jit(solution)/shard_map/ppermute | solution.py:27
  76.4 5.5 %copy-start.15 = (f32[2,8,32,128]{3,1,2,0:T(8,128)S(1)}, f32[2,8,32,128]{3,1,2,0:T(8,128)}, u32[]{:S(2)}) copy-start(f32[2,8,32,128]{3,1,2,0:T(8,128)} %get-tuple-element.41) | copy-start | bytes 786436
  77.5 4.5 %copy-start.33 = (bf16[1,2,2,128,128]{4,3,2,1,0:T(8,128)(2,1)S(1)}, bf16[1,2,2,128,128]{4,3,2,1,0:T(8,128)(2,1)}, u32[]{:S(2)}) copy-start(bf16[1,2,2,128,128]{4,3,2,1,0:T(8,128)(2,1)} %get-tuple-element.42) | copy-start | bytes 393220
  77.5 4.5 %copy-start.38 = (bf16[2,2,128,128]{3,2,1,0:T(8,128)(2,1)S(1)}, bf16[2,2,128,128]{3,2,1,0:T(8,128)(2,1)}, u32[]{:S(2)}) copy-start(bf16[2,2,128,128]{3,2,1,0:T(8,128)(2,1)} %copy-done.37) | copy-start | bytes 393220
  77.5 4.5 %copy-start.40 = (bf16[2,2,128,128]{3,2,1,0:T(8,128)(2,1)S(1)}, bf16[2,2,128,128]{3,2,1,0:T(8,128)(2,1)}, u32[]{:S(2)}) copy-start(bf16[2,2,128,128]{3,2,1,0:T(8,128)(2,1)} %copy-done.39) | copy-start | bytes 393220
  77.5 4.5 %copy-start.42 = (bf16[2,2,128,128]{3,2,1,0:T(8,128)(2,1)S(1)}, bf16[2,2,128,128]{3,2,1,0:T(8,128)(2,1)}, u32[]{:S(2)}) copy-start(bf16[2,2,128,128]{3,2,1,0:T(8,128)(2,1)} %copy-done.41) | copy-start | bytes 393220
  79.6 8.4 %copy-start.28 = (bf16[16,32,128]{2,1,0:T(8,128)(2,1)S(1)}, bf16[16,32,128]{2,1,0:T(8,128)(2,1)}, u32[]{:S(2)}) copy-start(bf16[16,32,128]{2,1,0:T(8,128)(2,1)} %copy-done.27) | copy-start | bytes 393220
  79.6 8.4 %copy-start.30 = (bf16[16,32,128]{2,1,0:T(8,128)(2,1)S(1)}, bf16[16,32,128]{2,1,0:T(8,128)(2,1)}, u32[]{:S(2)}) copy-start(bf16[16,32,128]{2,1,0:T(8,128)(2,1)} %copy-done.29) | copy-start | bytes 393220
  79.6 8.3 %copy-start.32 = (bf16[16,32,128]{2,1,0:T(8,128)(2,1)S(1)}, bf16[16,32,128]{2,1,0:T(8,128)(2,1)}, u32[]{:S(2)}) copy-start(bf16[16,32,128]{2,1,0:T(8,128)(2,1)} %copy-done.31) | copy-start | bytes 393220
  82.0 7.6 %copy-start.6 = (f32[128,4096]{1,0:T(8,128)S(1)}, f32[128,4096]{1,0:T(8,128)}, u32[]{:S(2)}) copy-start(f32[128,4096]{1,0:T(8,128)} %copy-done.5) | copy-start | bytes 6291460
  82.1 7.5 %copy-start.2 = (f32[2,8,32,128]{3,2,1,0:T(8,128)S(1)}, f32[2,8,32,128]{3,2,1,0:T(8,128)}, u32[]{:S(2)}) copy-start(f32[2,8,32,128]{3,2,1,0:T(8,128)} %copy.23) | copy-start | bytes 786436
  82.1 7.5 %copy-start.4 = (f32[128,4096]{1,0:T(8,128)S(1)}, f32[128,4096]{1,0:T(8,128)}, u32[]{:S(2)}) copy-start(f32[128,4096]{1,0:T(8,128)} %copy-done.3) | copy-start | bytes 6291460
  82.1 13.4 %collective-permute-start.15 = (bf16[4,2,2,128,128]{4,3,2,1,0:T(8,128)(2,1)S(1)}, bf16[4,2,2,128,128]{4,3,2,1,0:T(8,128)(2,1)S(1)}, u32[]{:S(2)}, u32[]{:S(2)}) collective-permute-start(bf16[4,2,2,128,128]{4,3,2,1,0:T(8,128)(2,1)S(1)} %pad_maximum_fusion.a0), channel_id=1, source_target_pairs={{0,16},{8,24},{16,0},{24,8},{1,17},{9,25},{17,1},{25,9},{2,18},{10... | collective-permute-start | bytes 1572872 | tf_op jit(solution)/shard_map/ppermute | solution.py:27
  86.0 23.6 %collective-permute-start.16 = (bf16[4,2,2,128,128]{4,3,2,1,0:T(8,128)(2,1)S(1)}, bf16[4,2,2,128,128]{4,3,2,1,0:T(8,128)(2,1)S(1)}, u32[]{:S(2)}, u32[]{:S(2)}) collective-permute-start(bf16[4,2,2,128,128]{4,3,2,1,0:T(8,128)(2,1)S(1)} %pad_maximum_fusion.a0), channel_id=1, source_target_pairs={{0,24},{8,0},{16,8},{24,16},{1,25},{9,1},{17,9},{25,17},{2,26},{10... | collective-permute-start | bytes 1572872 | tf_op jit(solution)/shard_map/ppermute | solution.py:27
  86.0 24.6 %collective-permute-start.22 = (bf16[4,2,2,128,128]{4,3,2,1,0:T(8,128)(2,1)S(1)}, bf16[4,2,2,128,128]{4,3,2,1,0:T(8,128)(2,1)S(1)}, u32[]{:S(2)}, u32[]{:S(2)}) collective-permute-start(bf16[4,2,2,128,128]{4,3,2,1,0:T(8,128)(2,1)S(1)} %pad_maximum_fusion.1.b0), channel_id=1, source_target_pairs={{0,2},{2,4},{4,6},{6,0},{1,3},{3,5},{5,7},{7,1},{8,10},{10,12},{12... | collective-permute-start | bytes 1572872 | tf_op jit(solution)/shard_map/ppermute | solution.py:27
  86.1 24.5 %collective-permute-start.23 = (bf16[4,2,2,128,128]{4,3,2,1,0:T(8,128)(2,1)S(1)}, bf16[4,2,2,128,128]{4,3,2,1,0:T(8,128)(2,1)S(1)}, u32[]{:S(2)}, u32[]{:S(2)}) collective-permute-start(bf16[4,2,2,128,128]{4,3,2,1,0:T(8,128)(2,1)S(1)} %pad_maximum_fusion.1.b0), channel_id=1, source_target_pairs={{0,4},{2,6},{4,0},{6,2},{1,5},{3,7},{5,1},{7,3},{8,12},{10,14},{12... | collective-permute-start | bytes 1572872 | tf_op jit(solution)/shard_map/ppermute | solution.py:27
  87.1 24.2 %collective-permute-start.24 = (bf16[4,2,2,128,128]{4,3,2,1,0:T(8,128)(2,1)S(1)}, bf16[4,2,2,128,128]{4,3,2,1,0:T(8,128)(2,1)S(1)}, u32[]{:S(2)}, u32[]{:S(2)}) collective-permute-start(bf16[4,2,2,128,128]{4,3,2,1,0:T(8,128)(2,1)S(1)} %pad_maximum_fusion.1.b0), channel_id=1, source_target_pairs={{0,6},{2,0},{4,2},{6,4},{1,7},{3,1},{5,3},{7,5},{8,14},{10,8},{12,... | collective-permute-start | bytes 1572872 | tf_op jit(solution)/shard_map/ppermute | solution.py:27
  89.6 5.9 %copy-start.35 = (bf16[128,1024]{1,0:T(8,128)(2,1)S(1)}, bf16[128,1024]{1,0:T(8,128)(2,1)}, u32[]{:S(2)}) copy-start(bf16[128,1024]{1,0:T(8,128)(2,1)} %get-tuple-element.18) | copy-start | bytes 786436
  89.6 20.0 %copy-start.34 = (bf16[128,1024]{1,0:T(8,128)(2,1)S(1)}, bf16[128,1024]{1,0:T(8,128)(2,1)}, u32[]{:S(2)}) copy-start(bf16[128,1024]{1,0:T(8,128)(2,1)} %get-tuple-element.15) | copy-start | bytes 786436
  89.6 21.7 %copy-start.11 = (s32[4]{0:T(128)S(1)}, s32[4]{0:T(128)}, u32[]{:S(2)}) copy-start(s32[4]{0:T(128)} %lengths_ref.7) | copy-start | bytes 52
  95.5 27.2 %collective-permute-start.27 = (bf16[128,1024]{1,0:T(8,128)(2,1)S(1)}, bf16[128,1024]{1,0:T(8,128)(2,1)S(1)}, u32[]{:S(2)}, u32[]{:S(2)}) collective-permute-start(bf16[128,1024]{1,0:T(8,128)(2,1)S(1)} %copy-done.35), channel_id=1, source_target_pairs={{0,64},{32,96},{64,0},{96,32},{1,65},{33,97},{65,1},{97,33},{2,66}... | collective-permute-start | bytes 786440 | tf_op jit(solution)/shard_map/ppermute | solution.py:27
  109.6 45.9 %collective-permute-start.29 = (bf16[128,1024]{1,0:T(8,128)(2,1)S(1)}, bf16[128,1024]{1,0:T(8,128)(2,1)S(1)}, u32[]{:S(2)}, u32[]{:S(2)}) collective-permute-start(bf16[128,1024]{1,0:T(8,128)(2,1)S(1)} %copy-done.34), channel_id=1, source_target_pairs={{0,96},{32,0},{64,32},{96,64},{1,97},{33,1},{65,33},{97,65},{2,98}... | collective-permute-start | bytes 786440 | tf_op jit(solution)/shard_map/ppermute | solution.py:27
  122.7 64.2 %collective-permute-start.26 = (bf16[128,1024]{1,0:T(8,128)(2,1)S(1)}, bf16[128,1024]{1,0:T(8,128)(2,1)S(1)}, u32[]{:S(2)}, u32[]{:S(2)}) collective-permute-start(bf16[128,1024]{1,0:T(8,128)(2,1)S(1)} %attend.5), channel_id=1, source_target_pairs={{0,96},{32,0},{64,32},{96,64},{1,97},{33,1},{65,33},{97,65},{2,98}... | collective-permute-start | bytes 786440 | tf_op jit(solution)/shard_map/ppermute | solution.py:27
  128.1 58.9 %collective-permute-start.28 = (bf16[128,1024]{1,0:T(8,128)(2,1)S(1)}, bf16[128,1024]{1,0:T(8,128)(2,1)S(1)}, u32[]{:S(2)}, u32[]{:S(2)}) collective-permute-start(bf16[128,1024]{1,0:T(8,128)(2,1)S(1)} %attend.6), channel_id=1, source_target_pairs={{0,64},{32,96},{64,0},{96,32},{1,65},{33,97},{65,1},{97,33},{2,66}... | collective-permute-start | bytes 786440 | tf_op jit(solution)/shard_map/ppermute | solution.py:27
  166.8 20.2 %collective-permute-start.30 = (bf16[128,1024]{1,0:T(8,128)(2,1)S(1)}, bf16[128,1024]{1,0:T(8,128)(2,1)S(1)}, u32[]{:S(2)}, u32[]{:S(2)}) collective-permute-start(bf16[128,1024]{1,0:T(8,128)(2,1)S(1)} %attend.7), channel_id=1, source_target_pairs={{0,32},{32,64},{64,96},{96,0},{1,33},{33,65},{65,97},{97,1},{2,34}... | collective-permute-start | bytes 786440 | tf_op jit(solution)/shard_map/ppermute | solution.py:27
  187.0 4.6 %copy-start.43 = (f32[4096]{0:T(1024)S(1)}, f32[4096]{0:T(1024)}, u32[]{:S(2)}) copy-start(f32[4096]{0:T(1024)} %param.14) | copy-start | bytes 49156
  188.0 5.0 %copy-start.12 = (bf16[128,4096]{1,0:T(8,128)(2,1)}, bf16[128,4096]{1,0:T(8,128)(2,1)S(1)}, u32[]{:S(2)}) copy-start(bf16[128,4096]{1,0:T(8,128)(2,1)S(1)} %get-tuple-element.10) | copy-start | bytes 3145732
  (11 other events, 21.7 us)
